TPU v7x, 128 devices: a whole 4x4x4 slice. The times are simulated.
128 devices in a mesh: shard: 64 (over z, y, x), grp: 2 (over core).
Axes of the slice: x: 4, y: 4, z: 4, core: 2. Of those that a mesh axis runs over, the one named last changes fastest.
Arguments:
- embeddings: bfloat16 [262144, 1024], P(('shard', 'grp'))
- send_row: int32 [128, 2048], P(('shard', 'grp')), may hold values from -1 to 2047, as said below
- slot_cluster: int32 [262144], P('shard'), may hold values from -1 to 15, as said below
Outputs:
- dup_score: float32 [262144], P(('shard', 'grp'))
Inputs may be any that keep to these rules, and one draw needn't show every extreme that they name: `send_row`: in each device's row, a local row index appears at most once; for destination d the used entries are the first ones, slots d * 16 to d * 16 + n - 1 with n from 1 to 16; some destination receives 16 rows from every device. slot_cluster[d * 2048 + s * 16 + k] is -1 exactly where send_row[s, d * 16 + k] is -1.
All inputs are finite; a program needn't handle non-finite values.
Results may differ from a plain program's by a relative error of at most 0.00031.
Values may be sent and summed in bfloat16 or wider, within the bound.
No kernel may reach another device: no remote copies, remote signals or barrier semaphores. Data moves between devices by JAX's collectives and lax.ppermute only.
A program may use at most 64 MiB of HBM per device.

v0:
```python
import jax
import jax.numpy as jnp
from jax import lax
from jax.sharding import PartitionSpec as P


def pair_max(left, left_labels, left_start, right, right_labels):
    rows_left = left.shape[0]
    count = right.shape[0]
    width = 512
    left_ids = left_start + jnp.arange(rows_left, dtype=jnp.int32)

    def advance(step, carry):
        row_best, col_best = carry
        begin = step * width
        block = lax.dynamic_slice_in_dim(right, begin, width, 0)
        labels = lax.dynamic_slice_in_dim(right_labels, begin, width, 0)
        ids = begin + jnp.arange(width, dtype=jnp.int32)
        scores = lax.dot_general(
            left, block, (((1,), (1,)), ((), ())), preferred_element_type=jnp.float32
        )
        keep = (
            (left_labels[:, None] == labels[None, :])
            & (left_labels[:, None] >= 0)
            & (left_ids[:, None] != ids[None, :])
        )
        masked = jnp.where(keep, scores, jnp.float32(-2.0))
        row_best = jnp.maximum(row_best, jnp.max(masked, axis=1))
        col_best = lax.dynamic_update_slice_in_dim(col_best, jnp.max(masked, axis=0), begin, 0)
        return (row_best, col_best)

    start_state = (jnp.full((rows_left,), -2.0, jnp.float32), jnp.full((count,), -2.0, jnp.float32))
    return lax.fori_loop(0, count // width, advance, start_state)


def per_device(embeddings, send_row, slot_cluster):
    rows = embeddings.shape[0]
    index_list = send_row[0]
    valid = index_list >= 0
    picked = jnp.take(embeddings, jnp.maximum(index_list, 0), axis=0).astype(jnp.float32)
    picked = jnp.where(valid[:, None], picked, 0.0)
    squares = lax.optimization_barrier(jnp.sum(picked * picked, axis=1, keepdims=True))
    unit = (picked * lax.rsqrt(squares + 1e-06)).astype(jnp.bfloat16)
    arrived = lax.all_to_all(unit, ("shard", "grp"), split_axis=0, concat_axis=0, tiled=True)
    mine = lax.axis_index("grp")
    own_start = mine * rows
    own_labels = lax.dynamic_slice_in_dim(slot_cluster, own_start, rows, 0)
    row_best, unused = pair_max(
        arrived,
        own_labels,
        own_start,
        lax.all_gather(arrived, "grp", axis=0, tiled=True),
        slot_cluster,
    )
    best = jnp.maximum(jnp.full((rows,), -2.0, jnp.float32), row_best)
    return jnp.maximum(best, jnp.float32(-1.0))


def solution(mesh):
    placed = (P(("shard", "grp"), None), P(("shard", "grp"), None), P("shard"))
    return jax.shard_map(
        per_device, mesh=mesh, in_specs=placed, out_specs=P(("shard", "grp")), check_vma=False
    )
```

profile of v0, /device:TPU:1, one launch (start us, length us, event | category | flops | bytes accessed | tf_op | source)
XLA Modules:
  0.0 164.5 jit_solution(14151223561534201431)
XLA Ops:
  6.5 0.0 all-gather.2.cloned.1.call-start
  6.5 0.8 compare_reduce_fusion.1
  7.3 0.7 broadcast_maximum_fusion
  8.0 0.1 ge.34
  8.1 0.1 le.20
  8.2 13.7 %gather_fusion = bf16[2048,1024]{1,0:T(8,128)(2,1)} fusion(bf16[2048,1024]{1,0:T(8,128)(2,1)} %param.5, s32[2048]{0:T(1024)S(1)} %broadcast_clamp_fusion), kind=kCustom, calls=%fused_computation | custom fusion | bytes 8396800 | tf_op jit(solution)/shard_map/jit(_take)/gather | solution.py:40
  21.9 3.6 %multiply_reduce_fusion = f32[2048]{0:T(1024)S(1)} fusion(bf16[2048,1024]{1,0:T(8,128)(2,1)} %gather_fusion, pred[2048]{0:T(1024)(128)(4,1)S(1)} %get-tuple-element.158, pred[2048]{0:T(1024)(128)(4,1)S(1)} %get-tuple-element.157), kind=kLoop, calls=%fused_computation.11 | loop fusion | flops 10483712 | bytes 4206592 | tf_op jit(solution)/shard_map/reduce_sum | solution.py:42
  25.6 0.1 mul.26
  25.6 3.9 %multiply_convert_fusion = bf16[128,16,1024]{2,1,0:T(8,128)(2,1)S(1)} fusion(f32[128,16]{1,0:T(8,128)S(1)} %mul.26, bf16[128,16,1024]{2,1,0:T(8,128)(2,1)} %bitcast.13, pred[128,16]{1,0:T(8,128)(4,1)S(1)} %le.20, pred[128,16]{1,0:T(8,128)(4,1)S(1)} %ge.34), kind=kLoop, calls=%fused_computation.10 | loop fusion | flops 10485760 | bytes 8400896 | tf_op jit(solution)/shard_map/convert_element_type | solution.py:43
  29.6 64.4 %all_to_all.9 = bf16[128,16,1024]{2,1,0:T(8,128)(2,1)} all-to-all(bf16[128,16,1024]{2,1,0:T(8,128)(2,1)S(1)} %multiply_convert_fusion), channel_id=1, replica_groups=mesh['shard'=64,'grp'=2] {'shard','grp'}, dimensions={0} | all-to-all | bytes 8388608 | tf_op jit(solution)/shard_map/all_to_all | solution.py:44
  94.0 0.0 copy-start
  94.0 0.0 all-gather.2.cloned.1.call-update
  94.0 0.7 copy-done
  94.7 18.0 %all-gather.2.cloned.1.call-done = bf16[4096,1024]{1,0:T(8,128)(2,1)} async-done(((bf16[2048,1024]{1,0:T(8,128)(2,1)}), bf16[4096,1024]{1,0:T(8,128)(2,1)}) %all-gather.2.cloned.1.call-update) | async-done | bytes 8388624 | tf_op jit(solution)/shard_map/all_gather | solution.py:52
  112.7 44.4 %while.14 = (s32[]{:T(128)}, f32[2048]{0:T(1024)S(1)}, s32[2048]{0:T(1024)S(1)}, s32[4096]{0:T(1024)S(1)}, bf16[4096,1024]{1,0:T(8,128)(2,1)}, /*index=5*/bf16[2...) while((s32[]{:T(128)}, f32[2048]{0:T(1024)S(1)}, ...), condition=%wide.region_3.4_spmd.clone, body=%wide.region_1.3_spmd.clone.sunk | while | flops 2153781760 | bytes 5322933 | solution.py:33
  112.7 0.1 dynamic_slice.25
  112.8 5.4 %fusion.11 = f32[2048]{0:T(1024)S(1)} fusion(bf16[2048,1024]{1,0:T(8,128)(2,1)} %get-tuple-element.243, s32[2048]{0:T(1024)S(1)} %iota_add_fusion.4, s32[2048]{0:T(1024)S(1)} %get-tuple-element.240, s32[512]{0:T(512)S(1)} %iota_add_fusion.5, s32[512]{0:T(512)S(1)} %dynamic_slice.25, pred[2048]{0:T(1024)(128)(4,1)S(1)} %broadcast_compare_fusion.2, ...), kind=kOutput, calls=%fused_computation.3.clone.1 | convolution fusion | flops 2153773056 | bytes 5273604 | tf_op jit(solution)/shard_map/while/body/eval_jaxpr/dot_general | solution.py:19
  118.2 0.1 dynamic_slice.25
  118.3 5.4 %fusion.11 = f32[2048]{0:T(1024)S(1)} fusion(bf16[2048,1024]{1,0:T(8,128)(2,1)} %get-tuple-element.243, s32[2048]{0:T(1024)S(1)} %iota_add_fusion.4, s32[2048]{0:T(1024)S(1)} %get-tuple-element.240, s32[512]{0:T(512)S(1)} %iota_add_fusion.5, s32[512]{0:T(512)S(1)} %dynamic_slice.25, pred[2048]{0:T(1024)(128)(4,1)S(1)} %broadcast_compare_fusion.2, ...), kind=kOutput, calls=%fused_computation.3.clone.1 | convolution fusion | flops 2153773056 | bytes 5273604 | tf_op jit(solution)/shard_map/while/body/eval_jaxpr/dot_general | solution.py:19
  123.8 0.1 dynamic_slice.25
  123.9 5.4 %fusion.11 = f32[2048]{0:T(1024)S(1)} fusion(bf16[2048,1024]{1,0:T(8,128)(2,1)} %get-tuple-element.243, s32[2048]{0:T(1024)S(1)} %iota_add_fusion.4, s32[2048]{0:T(1024)S(1)} %get-tuple-element.240, s32[512]{0:T(512)S(1)} %iota_add_fusion.5, s32[512]{0:T(512)S(1)} %dynamic_slice.25, pred[2048]{0:T(1024)(128)(4,1)S(1)} %broadcast_compare_fusion.2, ...), kind=kOutput, calls=%fused_computation.3.clone.1 | convolution fusion | flops 2153773056 | bytes 5273604 | tf_op jit(solution)/shard_map/while/body/eval_jaxpr/dot_general | solution.py:19
  129.3 0.1 dynamic_slice.25
  129.4 5.4 %fusion.11 = f32[2048]{0:T(1024)S(1)} fusion(bf16[2048,1024]{1,0:T(8,128)(2,1)} %get-tuple-element.243, s32[2048]{0:T(1024)S(1)} %iota_add_fusion.4, s32[2048]{0:T(1024)S(1)} %get-tuple-element.240, s32[512]{0:T(512)S(1)} %iota_add_fusion.5, s32[512]{0:T(512)S(1)} %dynamic_slice.25, pred[2048]{0:T(1024)(128)(4,1)S(1)} %broadcast_compare_fusion.2, ...), kind=kOutput, calls=%fused_computation.3.clone.1 | convolution fusion | flops 2153773056 | bytes 5273604 | tf_op jit(solution)/shard_map/while/body/eval_jaxpr/dot_general | solution.py:19
  134.9 0.1 dynamic_slice.25
  135.0 5.4 %fusion.11 = f32[2048]{0:T(1024)S(1)} fusion(bf16[2048,1024]{1,0:T(8,128)(2,1)} %get-tuple-element.243, s32[2048]{0:T(1024)S(1)} %iota_add_fusion.4, s32[2048]{0:T(1024)S(1)} %get-tuple-element.240, s32[512]{0:T(512)S(1)} %iota_add_fusion.5, s32[512]{0:T(512)S(1)} %dynamic_slice.25, pred[2048]{0:T(1024)(128)(4,1)S(1)} %broadcast_compare_fusion.2, ...), kind=kOutput, calls=%fused_computation.3.clone.1 | convolution fusion | flops 2153773056 | bytes 5273604 | tf_op jit(solution)/shard_map/while/body/eval_jaxpr/dot_general | solution.py:19
  140.4 0.1 dynamic_slice.25
  140.5 5.4 %fusion.11 = f32[2048]{0:T(1024)S(1)} fusion(bf16[2048,1024]{1,0:T(8,128)(2,1)} %get-tuple-element.243, s32[2048]{0:T(1024)S(1)} %iota_add_fusion.4, s32[2048]{0:T(1024)S(1)} %get-tuple-element.240, s32[512]{0:T(512)S(1)} %iota_add_fusion.5, s32[512]{0:T(512)S(1)} %dynamic_slice.25, pred[2048]{0:T(1024)(128)(4,1)S(1)} %broadcast_compare_fusion.2, ...), kind=kOutput, calls=%fused_computation.3.clone.1 | convolution fusion | flops 2153773056 | bytes 5273604 | tf_op jit(solution)/shard_map/while/body/eval_jaxpr/dot_general | solution.py:19
  146.0 0.1 dynamic_slice.25
  146.1 5.4 %fusion.11 = f32[2048]{0:T(1024)S(1)} fusion(bf16[2048,1024]{1,0:T(8,128)(2,1)} %get-tuple-element.243, s32[2048]{0:T(1024)S(1)} %iota_add_fusion.4, s32[2048]{0:T(1024)S(1)} %get-tuple-element.240, s32[512]{0:T(512)S(1)} %iota_add_fusion.5, s32[512]{0:T(512)S(1)} %dynamic_slice.25, pred[2048]{0:T(1024)(128)(4,1)S(1)} %broadcast_compare_fusion.2, ...), kind=kOutput, calls=%fused_computation.3.clone.1 | convolution fusion | flops 2153773056 | bytes 5273604 | tf_op jit(solution)/shard_map/while/body/eval_jaxpr/dot_general | solution.py:19
  151.5 0.1 dynamic_slice.25
  151.6 5.4 %fusion.11 = f32[2048]{0:T(1024)S(1)} fusion(bf16[2048,1024]{1,0:T(8,128)(2,1)} %get-tuple-element.243, s32[2048]{0:T(1024)S(1)} %iota_add_fusion.4, s32[2048]{0:T(1024)S(1)} %get-tuple-element.240, s32[512]{0:T(512)S(1)} %iota_add_fusion.5, s32[512]{0:T(512)S(1)} %dynamic_slice.25, pred[2048]{0:T(1024)(128)(4,1)S(1)} %broadcast_compare_fusion.2, ...), kind=kOutput, calls=%fused_computation.3.clone.1 | convolution fusion | flops 2153773056 | bytes 5273604 | tf_op jit(solution)/shard_map/while/body/eval_jaxpr/dot_general | solution.py:19
  157.1 0.6 maximum_maximum_fusion
  (36 shorter events, 0.2 us)
Async XLA Ops:
  6.5 106.2 %all-gather.2.cloned.1.call-start = ((), (), s32[]{:S(2)}) async-start(), calls=%async_computation.1 | async-start | bytes 12582912 | tf_op jit(solution)/shard_map/all_gather | solution.py:52
  94.0 0.7 copy-start
Sparse Core Ops, SparseCore 0:
  94.1 18.5 all-gather.1
where the time goes:
time: 165 us
  blocking collectives  64.4 us (39%)
  matrix products  43.3 us (26%)
  waiting for transfers between devices  18 us (11%)
  local copies, waits for them, and re-layouts  15.3 us (9%)
  between operations  13.5 us (8%)
  other arithmetic  9.76 us (6%)
    all_to_all x1, blocking collectives, per_device(): lax.all_to_all(unit, ('shard', 'grp'), split_axis=0, concat_axis=0, tiled...  64.4 us
    dot_general x8, matrix products, advance(): lax.dot_general(left, block, (((1,), (1,)), ((), ())), preferred_element_...  43.3 us
    all_gather x1, waiting for transfers between devices, per_device(): lax.all_gather(arrived, 'grp', axis=0, tiled=True)  18 us
    gather x1, local copies, waits for them, and re-layouts, per_device(): jnp.take(embeddings, jnp.maximum(index_list, 0), axis=0).astype(jnp.float32)  13.7 us
    convert_element_type x1, other arithmetic, per_device(): unit = (picked * lax.rsqrt(squares + 1e-06)).astype(jnp.bfloat16)  3.93 us
    reduce_sum x1, other arithmetic, per_device(): jnp.sum(picked * picked, axis=1, keepdims=True)  3.58 us
  transfers between devices with their start and end apart: 1, of which 1 were waited for; matrix products, arithmetic and copies ran while one was open for 0% of the time, Pallas kernels for 0%

commit v1 on v0

v1 whole, which is shorter than its diff:
```python
import functools

import jax
import jax.numpy as jnp
from jax import lax
from jax.experimental import pallas as pl
from jax.experimental.pallas import tpu as pltpu
from jax.sharding import PartitionSpec as P

LANES = 128
BLOCK = 256
VMEM_LIMIT = 56 << 20
ROWS_BY_ROWS = (((1,), (1,)), ((), ()))


def down_lanes(row):
    parts = [
        jnp.transpose(jnp.broadcast_to(row[:, j : j + LANES], (LANES, LANES)))
        for j in range(0, row.shape[1], LANES)
    ]
    return jnp.concatenate(parts, axis=0)


def fold_lanes(values):
    best = values[:, :LANES]
    for j in range(LANES, values.shape[1], LANES):
        best = jnp.maximum(best, values[:, j : j + LANES])
    return best


def across(values):
    parts = [
        jnp.max(jnp.transpose(values[i : i + LANES]), axis=0, keepdims=True)
        for i in range(0, values.shape[0], LANES)
    ]
    return jnp.concatenate(parts, axis=1)


def same_label(down, labels):
    return jnp.concatenate(
        [down == labels[:, j : j + LANES] for j in range(0, labels.shape[1], LANES)], axis=1
    )


def unit_rows_kernel(index_ref, rows_ref, unit_ref):
    total = rows_ref.shape[0]
    block = total // 2
    lane = lax.broadcasted_iota(jnp.int32, (block, LANES), 1)

    def step(b):
        start = pl.multiple_of(b * block, block)
        index = down_lanes(index_ref[:, pl.ds(start, block)])
        chosen = jnp.concatenate(
            [
                (index == lane + k).astype(jnp.float32).astype(jnp.bfloat16)
                for k in range(0, total, LANES)
            ],
            axis=1,
        )
        held = jnp.dot(chosen, rows_ref[...], preferred_element_type=jnp.float32)
        squares = jnp.sum(held * held, axis=1, keepdims=True)
        unit_ref[pl.ds(start, block), :] = (held * lax.rsqrt(squares + 1e-06)).astype(jnp.bfloat16)

    pl.loop(0, 2)(step)


def own_pairs_kernel(side_ref, labels_ref, own_ref, best_ref, fold_ref):
    rows = own_ref.shape[0]
    labels = labels_ref[:, pl.ds(pl.multiple_of(side_ref[0] * rows, rows), rows)]
    down = down_lanes(labels)
    along = jnp.where(labels < 0, -3, labels)
    fold_ref[...] = jnp.full(fold_ref.shape, -1.0, jnp.float32)
    for start in range(0, rows, BLOCK):
        height = start + BLOCK
        scores = lax.dot_general(
            own_ref[pl.ds(0, height), :],
            own_ref[pl.ds(start, BLOCK), :],
            ROWS_BY_ROWS,
            preferred_element_type=jnp.float32,
        )
        keep = same_label(down[:height], along[:, start : start + BLOCK])
        row_id = lax.broadcasted_iota(jnp.int32, (height, BLOCK), 0)
        column_id = lax.broadcasted_iota(jnp.int32, (height, BLOCK), 1) + start
        kept = jnp.where(keep & (row_id != column_id), scores, -1.0)
        best_ref[:, pl.ds(start, BLOCK)] = jnp.max(kept, axis=0, keepdims=True)
        part = pl.ds(0, height)
        fold_ref[part, :] = jnp.maximum(fold_ref[part, :], fold_lanes(kept))
    best_ref[...] = jnp.maximum(best_ref[...], across(fold_ref[...]))


def cross_pairs_kernel(side_ref, labels_ref, own_ref, other_ref, own_best_ref, other_best_ref):
    rows = own_ref.shape[0]
    half = rows // 2
    side = side_ref[0]
    for turn in range(2):
        mine = pl.multiple_of((side ^ turn) * half, half)
        own_labels = labels_ref[:, pl.ds(pl.multiple_of(side * rows + mine, half), half)]
        other_labels = labels_ref[
            :, pl.ds(pl.multiple_of((1 - side) * rows + turn * half, half), half)
        ]
        down = down_lanes(own_labels)
        along = jnp.where(other_labels < 0, -3, other_labels)
        fold = jnp.full((half, LANES), -1.0, jnp.float32)
        for start in range(0, half, BLOCK):
            scores = lax.dot_general(
                own_ref[pl.ds(mine, half), :],
                other_ref[pl.ds(turn * half + start, BLOCK), :],
                ROWS_BY_ROWS,
                preferred_element_type=jnp.float32,
            )
            kept = jnp.where(same_label(down, along[:, start : start + BLOCK]), scores, -1.0)
            other_best_ref[:, pl.ds(turn * half + start, BLOCK)] = jnp.max(
                kept, axis=0, keepdims=True
            )
            fold = jnp.maximum(fold, fold_lanes(kept))
        own_best_ref[:, pl.ds(mine, half)] = across(fold)


def vmem():
    return pl.BlockSpec(memory_space=pltpu.VMEM)


def smem():
    return pl.BlockSpec(memory_space=pltpu.SMEM)


def per_device(embeddings, send_row, slot_cluster):
    rows, width = embeddings.shape
    side = lax.axis_index("grp").astype(jnp.int32).reshape(1)
    labels = slot_cluster.reshape(1, -1)
    best_shape = jax.ShapeDtypeStruct((1, rows), jnp.float32)
    params = pltpu.CompilerParams(vmem_limit_bytes=VMEM_LIMIT)

    unit = pl.pallas_call(
        unit_rows_kernel,
        out_shape=jax.ShapeDtypeStruct((rows, width), jnp.bfloat16),
        in_specs=[vmem(), vmem()],
        out_specs=vmem(),
        compiler_params=params,
        cost_estimate=pl.CostEstimate(
            flops=2 * rows * rows * width, bytes_accessed=4 * rows * width, transcendentals=rows
        ),
        name="unit_rows",
    )(send_row, embeddings)

    own = lax.all_to_all(unit, ("shard", "grp"), split_axis=0, concat_axis=0, tiled=True)
    other = lax.ppermute(own, "grp", [(0, 1), (1, 0)])

    own_best = pl.pallas_call(
        own_pairs_kernel,
        out_shape=best_shape,
        in_specs=[smem(), vmem(), vmem()],
        out_specs=vmem(),
        scratch_shapes=[pltpu.VMEM((rows, LANES), jnp.float32)],
        compiler_params=params,
        cost_estimate=pl.CostEstimate(
            flops=rows * rows * width, bytes_accessed=2 * rows * width, transcendentals=0
        ),
        name="own_pairs",
    )(side, labels, own)

    cross_best, other_best = pl.pallas_call(
        cross_pairs_kernel,
        out_shape=[best_shape, best_shape],
        in_specs=[smem(), vmem(), vmem(), vmem()],
        out_specs=[vmem(), vmem()],
        compiler_params=params,
        cost_estimate=pl.CostEstimate(
            flops=rows * rows * width, bytes_accessed=4 * rows * width, transcendentals=0
        ),
        name="cross_pairs",
    )(side, labels, own, other)

    returned = lax.ppermute(other_best, "grp", [(0, 1), (1, 0)])
    best = jnp.maximum(jnp.maximum(own_best, cross_best), returned)
    return best.reshape(rows)


def solution(mesh):
    placed = (P(("shard", "grp"), None), P(("shard", "grp"), None), P("shard"))
    return jax.shard_map(
        per_device, mesh=mesh, in_specs=placed, out_specs=P(("shard", "grp")), check_vma=False
    )
```

time: 165 us -> 105 us (0.64)
  matrix products: 43.3 us -> 0 us
  Pallas kernels: 0 us -> 30.4 us
  local copies, waits for them, and re-layouts: 15.3 us -> 0.01 us
  between operations: 13.5 us -> 0.01 us
  waiting for transfers between devices: 18 us -> 7.13 us
  other arithmetic: 9.76 us -> 1.31 us
    dot_general x8 -> x0, matrix products: 43.3 us -> none  [advance(): lax.dot_general(left, block, (((1,), (1,)), ((), ())), preferred_element_...]
    pallas_call x0 -> x3, Pallas kernels: none -> 30.4 us  [the longest x1 13.6 us: per_device(): pl.pallas_call(unit_rows_kernel, out_shape=jax.ShapeDtypeStruct((rows, wi...]
    all_gather x1 -> x0, waiting for transfers between devices: 18 us -> none  [per_device(): lax.all_gather(arrived, 'grp', axis=0, tiled=True)]
    gather x1 -> x0, local copies, waits for them, and re-layouts: 13.7 us -> none  [per_device(): jnp.take(embeddings, jnp.maximum(index_list, 0), axis=0).astype(jnp.float32)]
    ppermute x0 -> x2, waiting for transfers between devices: none -> 7.13 us  [the longest x1 7.13 us: per_device(): other = lax.ppermute(own, 'grp', [(0, 1), (1, 0)])]
    convert_element_type x1 -> x0, other arithmetic: 3.93 us -> none  [per_device(): unit = (picked * lax.rsqrt(squares + 1e-06)).astype(jnp.bfloat16)]
    reduce_sum x1 -> x0, other arithmetic: 3.58 us -> none  [per_device(): jnp.sum(picked * picked, axis=1, keepdims=True)]
  transfers between devices with their start and end apart: 1 -> 2, of which waited for: 1 -> 1; matrix products, arithmetic and copies ran while one was open for 0% -> 0% of each run, Pallas kernels for 0% -> 8%
where the time goes in v1:
time: 105 us
  blocking collectives  64.6 us (62%)
  Pallas kernels  30.4 us (29%)
  waiting for transfers between devices  7.13 us (7%)
  other arithmetic  1.31 us (1%)
  starting transfers between devices  1.3 us (1%)
    all_to_all x1, blocking collectives, per_device(): lax.all_to_all(unit, ('shard', 'grp'), split_axis=0, concat_axis=0, tiled...  64.6 us
    pallas_call x1, Pallas kernels, per_device(): pl.pallas_call(unit_rows_kernel, out_shape=jax.ShapeDtypeStruct((rows, wi...  13.6 us
    pallas_call x1, Pallas kernels, per_device(): pl.pallas_call(cross_pairs_kernel, out_shape=[best_shape, best_shape], in...  8.77 us
    pallas_call x1, Pallas kernels, per_device(): pl.pallas_call(own_pairs_kernel, out_shape=best_shape, in_specs=[smem(),...  8.02 us
    ppermute x1, waiting for transfers between devices, per_device(): other = lax.ppermute(own, 'grp', [(0, 1), (1, 0)])  7.13 us
  transfers between devices with their start and end apart: 2, of which 1 were waited for; matrix products, arithmetic and copies ran while one was open for 0% of the time, Pallas kernels for 8%

profile of v1, /device:TPU:1, one launch (start us, length us, event | category | flops | bytes accessed | tf_op | source)
XLA Modules:
  0.0 104.8 jit_solution(11294168685757481103)
XLA Ops:
  0.0 13.6 %unit_rows.1 = bf16[2048,1024]{1,0:T(8,128)(2,1)} custom-call(s32[1,2048]{1,0:T(1,128)} %index_ref.1, bf16[2048,1024]{1,0:T(8,128)(2,1)} %rows_ref.1), custom_call_target="tpu_custom_call" | custom-call | flops 8589934592 | bytes 8388608 | tf_op jit(solution)/shard_map/unit_rows/pallas_call | solution.py:134
  13.6 64.6 %all_to_all.11 = bf16[128,16,1024]{2,1,0:T(8,128)(2,1)} all-to-all(bf16[128,16,1024]{2,1,0:T(8,128)(2,1)} %bitcast.5), channel_id=1, replica_groups=mesh['shard'=64,'grp'=2] {'shard','grp'}, dimensions={0} | all-to-all | bytes 8388608 | tf_op jit(solution)/shard_map/all_to_all | solution.py:146
  78.2 0.9 collective-permute-start
  79.2 7.1 %collective-permute-done.other_ref = bf16[2048,1024]{1,0:T(8,128)(2,1)} collective-permute-done((bf16[2048,1024]{1,0:T(8,128)(2,1)}, bf16[2048,1024]{1,0:T(8,128)(2,1)}, u32[]{:S(2)}, u32[]{:S(2)}) %collective-permute-start) | collective-permute-done | bytes 4194336 | tf_op jit(solution)/shard_map/ppermute | solution.py:147
  86.3 8.8 %cross_pairs.1 = (f32[1,2048]{1,0:T(1,128)}, f32[1,2048]{1,0:T(1,128)}) custom-call(s32[1]{0:T(128)} %bitcast.side_ref, s32[1,4096]{1,0:T(1,128)} %bitcast.6, bf16[2048,1024]{1,0:T(8,128)(2,1)} %bitcast.3.own_ref, bf16[2048,1024]{1,0:T(8,128)(2,1)} %collective-permute-done.other_ref), custom_call_target="tpu_custom_call" | custom-call | flops 4294967296 | bytes 8388608 | tf_op jit(solution)/shard_map/cross_pairs/pallas_call | solution.py:162
  95.1 0.0 copy-start
  95.1 0.4 collective-permute-start.1
  95.4 8.0 %own_pairs.1 = f32[1,2048]{1,0:T(1,128)} custom-call(s32[1]{0:T(128)} %bitcast.side_ref, s32[1,4096]{1,0:T(1,128)} %bitcast.7, bf16[2048,1024]{1,0:T(8,128)(2,1)} %bitcast.3.own_ref), custom_call_target="tpu_custom_call" | custom-call | flops 4294967296 | bytes 4194304 | tf_op jit(solution)/shard_map/own_pairs/pallas_call | solution.py:149
  103.5 0.0 collective-permute-done.1
  103.5 0.0 copy-done
  103.5 1.3 %maximum_maximum_fusion = f32[1,2048]{1,0:T(1,128)} fusion(f32[1,2048]{1,0:T(1,128)S(1)} %collective-permute-done.1, f32[1,2048]{1,0:T(1,128)} %own_pairs.1, f32[1,2048]{1,0:T(1,128)S(1)} %copy-done), kind=kLoop, calls=%fused_computation | loop fusion | flops 4096 | bytes 32768 | tf_op jit(solution)/shard_map/max | solution.py:175
Async XLA Ops:
  78.2 8.1 %collective-permute-start = (bf16[2048,1024]{1,0:T(8,128)(2,1)}, bf16[2048,1024]{1,0:T(8,128)(2,1)}, u32[]{:S(2)}, u32[]{:S(2)}) collective-permute-start(bf16[2048,1024]{1,0:T(8,128)(2,1)} %bitcast.3.own_ref), channel_id=1, source_target_pairs={{0,1},{1,0},{2,3},{3,2},{4,5},{5,4},{6,7},{7,6},{8,9},{9,8},{10,11... | collective-permute-start | bytes 12582920 | tf_op jit(solution)/shard_map/ppermute | solution.py:147
  95.1 8.4 %copy-start = (f32[1,2048]{1,0:T(1,128)S(1)}, f32[1,2048]{1,0:T(1,128)}, u32[]{:S(2)}) copy-start(f32[1,2048]{1,0:T(1,128)} %get-tuple-element.7) | copy-start | bytes 24580
  95.1 8.4 %collective-permute-start.1 = (f32[1,2048]{1,0:T(1,128)}, f32[1,2048]{1,0:T(1,128)S(1)}, u32[]{:S(2)}, u32[]{:S(2)}) collective-permute-start(f32[1,2048]{1,0:T(1,128)} %get-tuple-element.8), channel_id=1, source_target_pairs={{0,1},{1,0},{2,3},{3,2},{4,5},{5,4},{6,7},{7,6},{8,9},{9,8},{10,11... | collective-permute-start | bytes 24584 | tf_op jit(solution)/shard_map/ppermute | solution.py:174

commit v2 on v1

v2 whole, which is shorter than its diff:
```python
import jax
import jax.numpy as jnp
from jax import lax
from jax.experimental import pallas as pl
from jax.experimental.pallas import tpu as pltpu
from jax.sharding import PartitionSpec as P

LANES = 128
SUBLANES = 8
STRIDE = SUBLANES + 1
BLOCK = 256
PARTS = 2
SPAN = 1024
UNROLL = 128
ROWS_BY_ROWS = (((1,), (1,)), ((), ()))


def down_lanes(row):
    parts = [
        jnp.transpose(jnp.broadcast_to(row[:, j : j + LANES], (LANES, LANES)))
        for j in range(0, row.shape[1], LANES)
    ]
    return jnp.concatenate(parts, axis=0)


def fold_lanes(values):
    best = values[:, :LANES]
    for j in range(LANES, values.shape[1], LANES):
        best = jnp.maximum(best, values[:, j : j + LANES])
    return best


def across(values):
    parts = [
        jnp.max(jnp.transpose(values[i : i + LANES]), axis=0, keepdims=True)
        for i in range(0, values.shape[0], LANES)
    ]
    return jnp.concatenate(parts, axis=0)


def along_lanes(row):
    return jnp.concatenate([row[:, j : j + LANES] for j in range(0, row.shape[1], LANES)], axis=0)


def same_label(down, labels):
    return jnp.concatenate(
        [down == labels[:, j : j + LANES] for j in range(0, labels.shape[1], LANES)], axis=1
    )


def unit_rows_kernel(
    index_ref,
    rows_ref,
    unit_ref,
    rows_buf,
    unit_buf,
    source,
    target,
    squares,
    index_buf,
    place_buf,
    place_smem,
    index_sem,
    place_sem,
    in_sem,
    out_sem,
):
    rows, width = rows_ref.shape
    tiles = width // LANES
    group_in = (tiles + 1) * STRIDE
    group_out = tiles * STRIDE
    part = rows // PARTS

    def copy_in(p):
        span = pl.ds(p * part, part)
        return pltpu.make_async_copy(rows_ref.at[span, :], rows_buf.at[span, :], in_sem.at[p])

    def copy_out(p):
        span = pl.ds(p * part, part)
        return pltpu.make_async_copy(unit_buf.at[span, :], unit_ref.at[span, :], out_sem.at[p])

    copy_index = pltpu.make_async_copy(index_ref, index_buf, index_sem)
    copy_index.start()
    for p in range(PARTS):
        copy_in(p).start()
    empty = rows // SUBLANES * group_in
    source[pl.ds(empty, group_in), :] = jnp.zeros((group_in, LANES), jnp.float32)
    copy_place = pltpu.make_async_copy(place_buf, place_smem, place_sem)

    for p in range(PARTS):
        copy_in(p).wait()

        @pl.loop(0, part // UNROLL)
        def _(c):
            first = p * part + c * UNROLL
            held = rows_buf[pl.ds(pl.multiple_of(first, UNROLL), UNROLL), :].astype(jnp.float32)
            total = jnp.zeros((UNROLL, LANES), jnp.float32)
            for j in range(tiles):
                piece = held[:, j * LANES : (j + 1) * LANES]
                total = total + piece * piece
                for i in range(UNROLL // SUBLANES):
                    start = (first // SUBLANES + i) * group_in + j * STRIDE
                    source[pl.ds(start, SUBLANES), :] = piece[i * SUBLANES : (i + 1) * SUBLANES]
            squares[pl.ds(pl.multiple_of(first, UNROLL), UNROLL), :] = total

        if p == 0:
            copy_index.wait()
            index = index_buf[...]
            place_buf[...] = jnp.where(
                index < 0, empty, index + (index >> 3) * (group_in - SUBLANES)
            )
            copy_place.start()

    total = jnp.dot(
        squares[...],
        jnp.ones((LANES, LANES), jnp.float32),
        preferred_element_type=jnp.float32,
        precision=lax.Precision.HIGHEST,
    )
    scale = lax.rsqrt(total + 1e-06)
    for i in range(rows // SUBLANES):
        start = i * group_in + tiles * STRIDE
        source[pl.ds(start, SUBLANES), :] = scale[i * SUBLANES : (i + 1) * SUBLANES]
    copy_place.wait()

    for p in range(PARTS):

        @pl.loop(0, part // UNROLL)
        def _(c):
            first = p * part + c * UNROLL
            base = first // SUBLANES * group_out
            for s in range(UNROLL):
                place = place_smem[0, first + s]
                row = source[pl.ds(place, tiles, stride=STRIDE), :]
                scale = source[pl.ds(place + tiles * STRIDE, 1), :]
                start = base + s // SUBLANES * group_out + s % SUBLANES
                target[pl.ds(start, tiles, stride=STRIDE), :] = row * scale

        @pl.loop(0, part // UNROLL)
        def _(c):
            first = p * part + c * UNROLL
            base = first // SUBLANES * group_out
            groups = [
                jnp.concatenate(
                    [
                        target[pl.ds(base + i * group_out + j * STRIDE, SUBLANES), :]
                        for j in range(tiles)
                    ],
                    axis=1,
                )
                for i in range(UNROLL // SUBLANES)
            ]
            unit_buf[pl.ds(pl.multiple_of(first, UNROLL), UNROLL), :] = jnp.concatenate(
                groups, axis=0
            ).astype(jnp.bfloat16)

        copy_out(p).start()
    for p in range(PARTS):
        copy_out(p).wait()


def own_pairs_kernel(side_ref, labels_ref, own_hbm, best_ref, own_ref, fold_ref, sem):
    rows = own_ref.shape[0]
    copies = [
        pltpu.make_async_copy(
            own_hbm.at[pl.ds(start, SPAN), :], own_ref.at[pl.ds(start, SPAN), :], sem.at[i]
        )
        for i, start in enumerate(range(0, rows, SPAN))
    ]
    for copy in copies:
        copy.start()
    labels = labels_ref[:, pl.ds(pl.multiple_of(side_ref[0] * rows, rows), rows)]
    down = down_lanes(labels)
    along = jnp.where(labels < 0, -3, labels)
    fold_ref[...] = jnp.full(fold_ref.shape, -1.0, jnp.float32)
    columns = []
    for start in range(0, rows, BLOCK):
        if start % SPAN == 0:
            copies[start // SPAN].wait()
        height = start + BLOCK
        scores = lax.dot_general(
            own_ref[pl.ds(0, height), :],
            own_ref[pl.ds(start, BLOCK), :],
            ROWS_BY_ROWS,
            preferred_element_type=jnp.float32,
        )
        keep = same_label(down[:height], along[:, start : start + BLOCK])
        row_id = lax.broadcasted_iota(jnp.int32, (height, BLOCK), 0)
        column_id = lax.broadcasted_iota(jnp.int32, (height, BLOCK), 1) + start
        kept = jnp.where(keep & (row_id != column_id), scores, -1.0)
        columns.append(along_lanes(jnp.max(kept, axis=0, keepdims=True)))
        part = pl.ds(0, height)
        fold_ref[part, :] = jnp.maximum(fold_ref[part, :], fold_lanes(kept))
    best_ref[...] = jnp.maximum(jnp.concatenate(columns, axis=0), across(fold_ref[...]))


def cross_pairs_kernel(
    side_ref, labels_ref, best_ref, own_ref, other_hbm, own_best_ref, other_best_ref, other_ref, sem
):
    rows = own_ref.shape[0]
    half = rows // 2
    tiles = half // LANES
    side = side_ref[0]
    copies = [
        pltpu.make_async_copy(
            other_hbm.at[pl.ds(start, half), :], other_ref.at[pl.ds(start, half), :], sem.at[i]
        )
        for i, start in enumerate(range(0, rows, half))
    ]
    for copy in copies:
        copy.start()
    for turn in range(2):
        mine = side ^ turn
        first = pl.multiple_of(mine * half, half)
        own_labels = labels_ref[:, pl.ds(pl.multiple_of(side * rows + first, half), half)]
        other_labels = labels_ref[
            :, pl.ds(pl.multiple_of((1 - side) * rows + turn * half, half), half)
        ]
        down = down_lanes(own_labels)
        along = jnp.where(other_labels < 0, -3, other_labels)
        fold = jnp.full((half, LANES), -1.0, jnp.float32)
        columns = []
        copies[turn].wait()
        for start in range(0, half, BLOCK):
            scores = lax.dot_general(
                own_ref[pl.ds(first, half), :],
                other_ref[pl.ds(turn * half + start, BLOCK), :],
                ROWS_BY_ROWS,
                preferred_element_type=jnp.float32,
            )
            kept = jnp.where(same_label(down, along[:, start : start + BLOCK]), scores, -1.0)
            columns.append(along_lanes(jnp.max(kept, axis=0, keepdims=True)))
            fold = jnp.maximum(fold, fold_lanes(kept))
        other_best_ref[pl.ds(turn * tiles, tiles), :] = jnp.concatenate(columns, axis=0)
        part = pl.ds(pl.multiple_of(mine * tiles, tiles), tiles)
        own_best_ref[part, :] = jnp.maximum(best_ref[part, :], across(fold))


def vmem():
    return pl.BlockSpec(memory_space=pltpu.VMEM)


def smem():
    return pl.BlockSpec(memory_space=pltpu.SMEM)


def anywhere():
    return pl.BlockSpec(memory_space=pl.ANY)


def per_device(embeddings, send_row, slot_cluster):
    rows, width = embeddings.shape
    tiles = width // LANES
    groups = rows // SUBLANES
    side = lax.axis_index("grp").astype(jnp.int32).reshape(1)
    labels = slot_cluster.reshape(1, -1)
    row_shape = jax.ShapeDtypeStruct((rows, width), jnp.bfloat16)
    best_shape = jax.ShapeDtypeStruct((rows // LANES, LANES), jnp.float32)

    unit = pl.pallas_call(
        unit_rows_kernel,
        out_shape=row_shape,
        in_specs=[anywhere(), anywhere()],
        out_specs=anywhere(),
        scratch_shapes=[
            pltpu.VMEM((rows, width), jnp.bfloat16),
            pltpu.VMEM((rows, width), jnp.bfloat16),
            pltpu.VMEM(((groups + 1) * (tiles + 1) * STRIDE, LANES), jnp.float32),
            pltpu.VMEM((groups * tiles * STRIDE, LANES), jnp.float32),
            pltpu.VMEM((rows, LANES), jnp.float32),
            pltpu.VMEM((1, rows), jnp.int32),
            pltpu.VMEM((1, rows), jnp.int32),
            pltpu.SMEM((1, rows), jnp.int32),
            pltpu.SemaphoreType.DMA,
            pltpu.SemaphoreType.DMA,
            pltpu.SemaphoreType.DMA((PARTS,)),
            pltpu.SemaphoreType.DMA((PARTS,)),
        ],
        compiler_params=pltpu.CompilerParams(vmem_limit_bytes=60 << 20),
        cost_estimate=pl.CostEstimate(
            flops=8 * rows * width, bytes_accessed=4 * rows * width, transcendentals=rows
        ),
        name="unit_rows",
    )(send_row, embeddings)

    own = lax.all_to_all(unit, ("shard", "grp"), split_axis=0, concat_axis=0, tiled=True)
    other = lax.ppermute(own, "grp", [(0, 1), (1, 0)])

    own_best, own_kept = pl.pallas_call(
        own_pairs_kernel,
        out_shape=[best_shape, row_shape],
        in_specs=[smem(), vmem(), anywhere()],
        out_specs=[vmem(), vmem()],
        scratch_shapes=[
            pltpu.VMEM((rows, LANES), jnp.float32),
            pltpu.SemaphoreType.DMA((rows // SPAN,)),
        ],
        compiler_params=pltpu.CompilerParams(vmem_limit_bytes=26 << 20),
        cost_estimate=pl.CostEstimate(
            flops=rows * rows * width, bytes_accessed=2 * rows * width, transcendentals=0
        ),
        name="own_pairs",
    )(side, labels, own)

    own_best, other_best = pl.pallas_call(
        cross_pairs_kernel,
        out_shape=[best_shape, best_shape],
        in_specs=[smem(), vmem(), vmem(), vmem(), anywhere()],
        out_specs=[vmem(), vmem()],
        scratch_shapes=[
            pltpu.VMEM((rows, width), jnp.bfloat16),
            pltpu.SemaphoreType.DMA((2,)),
        ],
        compiler_params=pltpu.CompilerParams(vmem_limit_bytes=26 << 20),
        cost_estimate=pl.CostEstimate(
            flops=rows * rows * width, bytes_accessed=4 * rows * width, transcendentals=0
        ),
        name="cross_pairs",
    )(side, labels, own_best, own_kept, other)

    returned = lax.ppermute(other_best, "grp", [(0, 1), (1, 0)])
    return jnp.maximum(own_best, returned).reshape(rows)


def solution(mesh):
    placed = (P(("shard", "grp"), None), P(("shard", "grp"), None), P("shard"))
    return jax.shard_map(
        per_device, mesh=mesh, in_specs=placed, out_specs=P(("shard", "grp")), check_vma=False
    )
```

time: 105 us -> 90.1 us (0.86)
  Pallas kernels: 30.4 us -> 22.4 us
  waiting for transfers between devices: 7.13 us -> 1.16 us
    ppermute x1, waiting for transfers between devices: 7.13 us -> 0.01 us  [per_device(): other = lax.ppermute(own, 'grp', [(0, 1), (1, 0)])]
    pallas_call x2, Pallas kernels: 21.7 us -> 15.8 us  [the longest x1 7.94 us: per_device(): pl.pallas_call(unit_rows_kernel, out_shape=row_shape, in_specs=[anywhere(...]
    pallas_call x1, Pallas kernels: 8.77 us -> 6.62 us  [per_device(): pl.pallas_call(cross_pairs_kernel, out_shape=[best_shape, best_shape], in...]
    max x1 -> x0, other arithmetic: 1.31 us -> none  [per_device(): best = jnp.maximum(jnp.maximum(own_best, cross_best), returned)]
    ppermute x1, waiting for transfers between devices: 0.01 us -> 1.16 us  [per_device(): returned = lax.ppermute(other_best, 'grp', [(0, 1), (1, 0)])]
  transfers between devices with their start and end apart: 2 -> 2, of which waited for: 1 -> 1; matrix products, arithmetic and copies ran while one was open for 0% -> 0% of each run, Pallas kernels for 8% -> 9%
where the time goes in v2:
time: 90.1 us; the launch traced here: 89.9 us
  blocking collectives  64.6 us (72%)
  Pallas kernels  22.4 us (25%)
  waiting for transfers between devices  1.16 us (1%)
  starting transfers between devices  1.02 us (1%)
    all_to_all x1, blocking collectives, per_device(): lax.all_to_all(unit, ('shard', 'grp'), split_axis=0, concat_axis=0, tiled...  64.6 us
    pallas_call x1, Pallas kernels, per_device(): pl.pallas_call(unit_rows_kernel, out_shape=row_shape, in_specs=[anywhere(...  7.94 us
    pallas_call x1, Pallas kernels, per_device(): pl.pallas_call(own_pairs_kernel, out_shape=[best_shape, row_shape], in_sp...  7.84 us
    pallas_call x1, Pallas kernels, per_device(): pl.pallas_call(cross_pairs_kernel, out_shape=[best_shape, best_shape], in...  6.62 us
  transfers between devices with their start and end apart: 2, of which 1 were waited for; matrix products, arithmetic and copies ran while one was open for 0% of the time, Pallas kernels for 9%

profile of v2, /device:TPU:1, one launch (start us, length us, event | category | flops | bytes accessed | tf_op | source)
XLA Modules:
  0.0 89.9 jit_solution(16781417688665936037)
XLA Ops:
  0.0 7.9 %unit_rows.1 = bf16[2048,1024]{1,0:T(8,128)(2,1)} custom-call(s32[1,2048]{1,0:T(1,128)} %index_ref.1, bf16[2048,1024]{1,0:T(8,128)(2,1)} %rows_ref.1), custom_call_target="tpu_custom_call" | custom-call | flops 16777216 | bytes 8388608 | tf_op jit(solution)/shard_map/unit_rows/pallas_call | solution.py:260
  8.0 0.0 copy-start
  8.0 64.6 %all_to_all.11 = bf16[128,16,1024]{2,1,0:T(8,128)(2,1)} all-to-all(bf16[128,16,1024]{2,1,0:T(8,128)(2,1)} %bitcast.8), channel_id=1, replica_groups=mesh['shard'=64,'grp'=2] {'shard','grp'}, dimensions={0} | all-to-all | bytes 8388608 | tf_op jit(solution)/shard_map/all_to_all | solution.py:286
  72.6 0.9 %collective-permute-start = (bf16[2048,1024]{1,0:T(8,128)(2,1)}, bf16[2048,1024]{1,0:T(8,128)(2,1)}, u32[]{:S(2)}, u32[]{:S(2)}) collective-permute-start(bf16[2048,1024]{1,0:T(8,128)(2,1)} %bitcast.3.own_hbm), channel_id=1, source_target_pairs={{0,1},{1,0},{2,3},{3,2},{4,5},{5,4},{6,7},{7,6},{8,9},{9,8},{10,11... | collective-permute-start | bytes 12582920 | tf_op jit(solution)/shard_map/ppermute | solution.py:287
  73.5 0.0 copy-done
  73.5 7.8 %own_pairs.1 = (f32[16,128]{1,0:T(8,128)S(1)}, bf16[2048,1024]{1,0:T(8,128)(2,1)S(1)}) custom-call(s32[1]{0:T(128)} %bitcast.side_ref, s32[1,4096]{1,0:T(1,128)S(1)} %bitcast.6, bf16[2048,1024]{1,0:T(8,128)(2,1)} %bitcast.3.own_hbm), custom_call_target="tpu_custom_call" | custom-call | flops 4294967296 | bytes 4194304 | tf_op jit(solution)/shard_map/own_pairs/pallas_call | solution.py:289
  81.4 0.0 collective-permute-done.other_hbm
  81.4 6.6 %cross_pairs.1 = (f32[16,128]{1,0:T(8,128)S(1)}, f32[16,128]{1,0:T(8,128)S(1)}) custom-call(s32[1]{0:T(128)} %bitcast.side_ref, s32[1,4096]{1,0:T(1,128)S(1)} %bitcast.7, f32[16,128]{1,0:T(8,128)S(1)} %get-tuple-element.9.best_ref, bf16[2048,1024]{1,0:T(8,128)(2,1)S(1)} %get-tuple-element.10.own_ref, bf16[2048,1024]{1,0:T(8,128)(2,1)} %collective-permute-done.other_hbm), custom_call_target="tpu_custom_call" | custom-call | flops 4294967296 | bytes 8388608 | tf_op jit(solution)/shard_map/cross_pairs/pallas_call | solution.py:305
  88.0 0.1 collective-permute-start.1
  88.1 1.2 %collective-permute-done.1 = f32[16,128]{1,0:T(8,128)S(1)} collective-permute-done((f32[16,128]{1,0:T(8,128)S(1)}, f32[16,128]{1,0:T(8,128)S(1)}, u32[]{:S(2)}, u32[]{:S(2)}) %collective-permute-start.1) | collective-permute-done | bytes 8224 | tf_op jit(solution)/shard_map/ppermute | solution.py:321
  89.3 0.6 maximum_bitcast_fusion
Async XLA Ops:
  8.0 65.6 %copy-start = (s32[4096]{0:T(1024)S(1)}, s32[4096]{0:T(1024)}, u32[]{:S(2)}) copy-start(s32[4096]{0:T(1024)} %param.5) | copy-start | bytes 49156
  72.6 8.8 %collective-permute-start = (bf16[2048,1024]{1,0:T(8,128)(2,1)}, bf16[2048,1024]{1,0:T(8,128)(2,1)}, u32[]{:S(2)}, u32[]{:S(2)}) collective-permute-start(bf16[2048,1024]{1,0:T(8,128)(2,1)} %bitcast.3.own_hbm), channel_id=1, source_target_pairs={{0,1},{1,0},{2,3},{3,2},{4,5},{5,4},{6,7},{7,6},{8,9},{9,8},{10,11... | collective-permute-start | bytes 12582920 | tf_op jit(solution)/shard_map/ppermute | solution.py:287
  88.0 1.3 %collective-permute-start.1 = (f32[16,128]{1,0:T(8,128)S(1)}, f32[16,128]{1,0:T(8,128)S(1)}, u32[]{:S(2)}, u32[]{:S(2)}) collective-permute-start(f32[16,128]{1,0:T(8,128)S(1)} %get-tuple-element.12), channel_id=1, source_target_pairs={{0,1},{1,0},{2,3},{3,2},{4,5},{5,4},{6,7},{7,6},{8,9},{9,8},{10,11... | collective-permute-start | bytes 24584 | tf_op jit(solution)/shard_map/ppermute | solution.py:321

commit v3 on v2

--- a/solution.py
+++ b/solution.py
@@ -9,7 +9,7 @@
 SUBLANES = 8
 STRIDE = SUBLANES + 1
 BLOCK = 256
-PARTS = 2
+PARTS = 4
 SPAN = 1024
 UNROLL = 128
 ROWS_BY_ROWS = (((1,), (1,)), ((), ()))
@@ -42,10 +42,14 @@
     return jnp.concatenate([row[:, j : j + LANES] for j in range(0, row.shape[1], LANES)], axis=0)
 
 
-def same_label(down, labels):
-    return jnp.concatenate(
-        [down == labels[:, j : j + LANES] for j in range(0, labels.shape[1], LANES)], axis=1
-    )
+def add_lanes(values):
+    terms = []
+    for _ in range(3):
+        term = values.astype(jnp.bfloat16)
+        terms.append(term)
+        values = values - term.astype(jnp.float32)
+    ones = jnp.ones((3 * LANES, LANES), jnp.bfloat16)
+    return jnp.dot(jnp.concatenate(terms, axis=1), ones, preferred_element_type=jnp.float32)
 
 
 def unit_rows_kernel(
@@ -53,7 +57,6 @@
     rows_ref,
     unit_ref,
     rows_buf,
-    unit_buf,
     source,
     target,
     squares,
@@ -63,7 +66,6 @@
     index_sem,
     place_sem,
     in_sem,
-    out_sem,
 ):
     rows, width = rows_ref.shape
     tiles = width // LANES
@@ -74,10 +76,6 @@
     def copy_in(p):
         span = pl.ds(p * part, part)
         return pltpu.make_async_copy(rows_ref.at[span, :], rows_buf.at[span, :], in_sem.at[p])
-
-    def copy_out(p):
-        span = pl.ds(p * part, part)
-        return pltpu.make_async_copy(unit_buf.at[span, :], unit_ref.at[span, :], out_sem.at[p])
 
     copy_index = pltpu.make_async_copy(index_ref, index_buf, index_sem)
     copy_index.start()
@@ -92,8 +90,8 @@
 
         @pl.loop(0, part // UNROLL)
         def _(c):
-            first = p * part + c * UNROLL
-            held = rows_buf[pl.ds(pl.multiple_of(first, UNROLL), UNROLL), :].astype(jnp.float32)
+            first = pl.multiple_of(p * part + c * UNROLL, UNROLL)
+            held = rows_buf[pl.ds(first, UNROLL), :].astype(jnp.float32)
             total = jnp.zeros((UNROLL, LANES), jnp.float32)
             for j in range(tiles):
                 piece = held[:, j * LANES : (j + 1) * LANES]
@@ -101,7 +99,7 @@
                 for i in range(UNROLL // SUBLANES):
                     start = (first // SUBLANES + i) * group_in + j * STRIDE
                     source[pl.ds(start, SUBLANES), :] = piece[i * SUBLANES : (i + 1) * SUBLANES]
-            squares[pl.ds(pl.multiple_of(first, UNROLL), UNROLL), :] = total
+            squares[pl.ds(first, UNROLL), :] = total
 
         if p == 0:
             copy_index.wait()
@@ -111,52 +109,59 @@
             )
             copy_place.start()
 
-    total = jnp.dot(
-        squares[...],
-        jnp.ones((LANES, LANES), jnp.float32),
-        preferred_element_type=jnp.float32,
-        precision=lax.Precision.HIGHEST,
-    )
-    scale = lax.rsqrt(total + 1e-06)
+    scale = lax.rsqrt(add_lanes(squares[...]) + 1e-06)
     for i in range(rows // SUBLANES):
         start = i * group_in + tiles * STRIDE
         source[pl.ds(start, SUBLANES), :] = scale[i * SUBLANES : (i + 1) * SUBLANES]
     copy_place.wait()
 
-    for p in range(PARTS):
-
-        @pl.loop(0, part // UNROLL)
-        def _(c):
-            first = p * part + c * UNROLL
-            base = first // SUBLANES * group_out
-            for s in range(UNROLL):
-                place = place_smem[0, first + s]
-                row = source[pl.ds(place, tiles, stride=STRIDE), :]
-                scale = source[pl.ds(place + tiles * STRIDE, 1), :]
-                start = base + s // SUBLANES * group_out + s % SUBLANES
-                target[pl.ds(start, tiles, stride=STRIDE), :] = row * scale
-
-        @pl.loop(0, part // UNROLL)
-        def _(c):
-            first = p * part + c * UNROLL
-            base = first // SUBLANES * group_out
-            groups = [
-                jnp.concatenate(
-                    [
-                        target[pl.ds(base + i * group_out + j * STRIDE, SUBLANES), :]
-                        for j in range(tiles)
-                    ],
-                    axis=1,
-                )
-                for i in range(UNROLL // SUBLANES)
-            ]
-            unit_buf[pl.ds(pl.multiple_of(first, UNROLL), UNROLL), :] = jnp.concatenate(
-                groups, axis=0
-            ).astype(jnp.bfloat16)
-
-        copy_out(p).start()
-    for p in range(PARTS):
-        copy_out(p).wait()
+    def move(first):
+        base = first // SUBLANES * group_out
+        for s in range(UNROLL):
+            place = place_smem[0, first + s]
+            row = source[pl.ds(place, tiles, stride=STRIDE), :]
+            factor = source[pl.ds(place + tiles * STRIDE, 1), :]
+            start = base + s // SUBLANES * group_out + s % SUBLANES
+            target[pl.ds(start, tiles, stride=STRIDE), :] = row * factor
+
+    def write(first):
+        base = first // SUBLANES * group_out
+        groups = []
+        for i in range(UNROLL // SUBLANES):
+            start = base + i * group_out
+            pieces = [target[pl.ds(start + j * STRIDE, SUBLANES), :] for j in range(tiles)]
+            groups.append(jnp.concatenate(pieces, axis=1))
+        unit_ref[pl.ds(pl.multiple_of(first, UNROLL), UNROLL), :] = jnp.concatenate(
+            groups, axis=0
+        ).astype(jnp.bfloat16)
+
+    move(0)
+
+    @pl.loop(1, rows // UNROLL)
+    def _(c):
+        write((c - 1) * UNROLL)
+        move(c * UNROLL)
+
+    write(rows - UNROLL)
+
+
+def matched(left, right, down, along):
+    scores = lax.dot_general(left, right, ROWS_BY_ROWS, preferred_element_type=jnp.float32)
+    keep = [down == along[:, j : j + LANES] for j in range(0, along.shape[1], LANES)]
+    return jnp.where(jnp.concatenate(keep, axis=1), scores, -1.0)
+
+
+def own_column(own_ref, down, along, start):
+    height = start + BLOCK
+    kept = matched(
+        own_ref[pl.ds(0, height), :],
+        own_ref[pl.ds(start, BLOCK), :],
+        down[:height],
+        along[:, start : start + BLOCK],
+    )
+    row_id = lax.broadcasted_iota(jnp.int32, (height, BLOCK), 0)
+    column_id = lax.broadcasted_iota(jnp.int32, (height, BLOCK), 1) + start
+    return jnp.where(row_id != column_id, kept, -1.0)
 
 
 def own_pairs_kernel(side_ref, labels_ref, own_hbm, best_ref, own_ref, fold_ref, sem):
@@ -177,19 +182,9 @@
     for start in range(0, rows, BLOCK):
         if start % SPAN == 0:
             copies[start // SPAN].wait()
-        height = start + BLOCK
-        scores = lax.dot_general(
-            own_ref[pl.ds(0, height), :],
-            own_ref[pl.ds(start, BLOCK), :],
-            ROWS_BY_ROWS,
-            preferred_element_type=jnp.float32,
-        )
-        keep = same_label(down[:height], along[:, start : start + BLOCK])
-        row_id = lax.broadcasted_iota(jnp.int32, (height, BLOCK), 0)
-        column_id = lax.broadcasted_iota(jnp.int32, (height, BLOCK), 1) + start
-        kept = jnp.where(keep & (row_id != column_id), scores, -1.0)
+        kept = own_column(own_ref, down, along, start)
         columns.append(along_lanes(jnp.max(kept, axis=0, keepdims=True)))
-        part = pl.ds(0, height)
+        part = pl.ds(0, start + BLOCK)
         fold_ref[part, :] = jnp.maximum(fold_ref[part, :], fold_lanes(kept))
     best_ref[...] = jnp.maximum(jnp.concatenate(columns, axis=0), across(fold_ref[...]))
 
@@ -209,6 +204,7 @@
     ]
     for copy in copies:
         copy.start()
+
     for turn in range(2):
         mine = side ^ turn
         first = pl.multiple_of(mine * half, half)
@@ -222,13 +218,12 @@
         columns = []
         copies[turn].wait()
         for start in range(0, half, BLOCK):
-            scores = lax.dot_general(
+            kept = matched(
                 own_ref[pl.ds(first, half), :],
                 other_ref[pl.ds(turn * half + start, BLOCK), :],
-                ROWS_BY_ROWS,
-                preferred_element_type=jnp.float32,
+                down,
+                along[:, start : start + BLOCK],
             )
-            kept = jnp.where(same_label(down, along[:, start : start + BLOCK]), scores, -1.0)
             columns.append(along_lanes(jnp.max(kept, axis=0, keepdims=True)))
             fold = jnp.maximum(fold, fold_lanes(kept))
         other_best_ref[pl.ds(turn * tiles, tiles), :] = jnp.concatenate(columns, axis=0)
@@ -259,11 +254,10 @@
 
     unit = pl.pallas_call(
         unit_rows_kernel,
-        out_shape=row_shape,
+        out_shape=pltpu.VMEM((rows, width), jnp.bfloat16),
         in_specs=[anywhere(), anywhere()],
-        out_specs=anywhere(),
+        out_specs=vmem(),
         scratch_shapes=[
-            pltpu.VMEM((rows, width), jnp.bfloat16),
             pltpu.VMEM((rows, width), jnp.bfloat16),
             pltpu.VMEM(((groups + 1) * (tiles + 1) * STRIDE, LANES), jnp.float32),
             pltpu.VMEM((groups * tiles * STRIDE, LANES), jnp.float32),
@@ -274,9 +268,8 @@
             pltpu.SemaphoreType.DMA,
             pltpu.SemaphoreType.DMA,
             pltpu.SemaphoreType.DMA((PARTS,)),
-            pltpu.SemaphoreType.DMA((PARTS,)),
         ],
-        compiler_params=pltpu.CompilerParams(vmem_limit_bytes=60 << 20),
+        compiler_params=pltpu.CompilerParams(vmem_limit_bytes=59 << 20),
         cost_estimate=pl.CostEstimate(
             flops=8 * rows * width, bytes_accessed=4 * rows * width, transcendentals=rows
         ),

time: 90.1 us -> 87.6 us (0.972)
  Pallas kernels: 22.4 us -> 20.2 us
    pallas_call x1, Pallas kernels: 7.94 us -> 5.66 us  [per_device(): pl.pallas_call(unit_rows_kernel, out_shape=pltpu.VMEM((rows, width), jnp....]
where the time goes in v3:
time: 87.6 us; the launch traced here: 87.4 us
  blocking collectives  64.4 us (74%)
  Pallas kernels  20.2 us (23%)
  waiting for transfers between devices  1.16 us (1%)
  starting transfers between devices  1.02 us (1%)
    all_to_all x1, blocking collectives, per_device(): lax.all_to_all(unit, ('shard', 'grp'), split_axis=0, concat_axis=0, tiled...  64.4 us
    pallas_call x1, Pallas kernels, per_device(): pl.pallas_call(own_pairs_kernel, out_shape=[best_shape, row_shape], in_sp...  7.85 us
    pallas_call x1, Pallas kernels, per_device(): pl.pallas_call(cross_pairs_kernel, out_shape=[best_shape, best_shape], in...  6.66 us
    pallas_call x1, Pallas kernels, per_device(): pl.pallas_call(unit_rows_kernel, out_shape=pltpu.VMEM((rows, width), jnp....  5.66 us
  transfers between devices with their start and end apart: 2, of which 1 were waited for; matrix products, arithmetic and copies ran while one was open for 0% of the time, Pallas kernels for 9%

profile of v3, /device:TPU:1, one launch (start us, length us, event | category | flops | bytes accessed | tf_op | source)
XLA Modules:
  0.0 87.4 jit_solution(1498054165230541283)
XLA Ops:
  0.0 5.7 %unit_rows.1 = bf16[2048,1024]{1,0:T(8,128)(2,1)S(1)} custom-call(s32[1,2048]{1,0:T(1,128)} %index_ref.1, bf16[2048,1024]{1,0:T(8,128)(2,1)} %rows_ref.1), custom_call_target="tpu_custom_call" | custom-call | flops 16777216 | bytes 8388608 | tf_op jit(solution)/shard_map/unit_rows/pallas_call | solution.py:255
  5.7 0.0 copy-start
  5.7 64.4 %all_to_all.11 = bf16[128,16,1024]{2,1,0:T(8,128)(2,1)} all-to-all(bf16[128,16,1024]{2,1,0:T(8,128)(2,1)S(1)} %bitcast.6), channel_id=1, replica_groups=mesh['shard'=64,'grp'=2] {'shard','grp'}, dimensions={0} | all-to-all | bytes 8388608 | tf_op jit(solution)/shard_map/all_to_all | solution.py:279
  70.1 0.9 %collective-permute-start = (bf16[2048,1024]{1,0:T(8,128)(2,1)}, bf16[2048,1024]{1,0:T(8,128)(2,1)}, u32[]{:S(2)}, u32[]{:S(2)}) collective-permute-start(bf16[2048,1024]{1,0:T(8,128)(2,1)} %bitcast.3.own_hbm), channel_id=1, source_target_pairs={{0,1},{1,0},{2,3},{3,2},{4,5},{5,4},{6,7},{7,6},{8,9},{9,8},{10,11... | collective-permute-start | bytes 12582920 | tf_op jit(solution)/shard_map/ppermute | solution.py:280
  71.0 0.0 copy-done
  71.0 7.9 %own_pairs.1 = (f32[16,128]{1,0:T(8,128)S(1)}, bf16[2048,1024]{1,0:T(8,128)(2,1)S(1)}) custom-call(s32[1]{0:T(128)} %bitcast.side_ref, s32[1,4096]{1,0:T(1,128)S(1)} %bitcast.7, bf16[2048,1024]{1,0:T(8,128)(2,1)} %bitcast.3.own_hbm), custom_call_target="tpu_custom_call" | custom-call | flops 4294967296 | bytes 4194304 | tf_op jit(solution)/shard_map/own_pairs/pallas_call | solution.py:282
  78.9 0.0 collective-permute-done.other_hbm
  78.9 6.7 %cross_pairs.1 = (f32[16,128]{1,0:T(8,128)S(1)}, f32[16,128]{1,0:T(8,128)S(1)}) custom-call(s32[1]{0:T(128)} %bitcast.side_ref, s32[1,4096]{1,0:T(1,128)S(1)} %bitcast.8, f32[16,128]{1,0:T(8,128)S(1)} %get-tuple-element.9.best_ref, bf16[2048,1024]{1,0:T(8,128)(2,1)S(1)} %get-tuple-element.10.own_ref, bf16[2048,1024]{1,0:T(8,128)(2,1)} %collective-permute-done.other_hbm), custom_call_target="tpu_custom_call" | custom-call | flops 4294967296 | bytes 8388608 | tf_op jit(solution)/shard_map/cross_pairs/pallas_call | solution.py:298
  85.6 0.1 collective-permute-start.1
  85.6 1.2 %collective-permute-done.1 = f32[16,128]{1,0:T(8,128)S(1)} collective-permute-done((f32[16,128]{1,0:T(8,128)S(1)}, f32[16,128]{1,0:T(8,128)S(1)}, u32[]{:S(2)}, u32[]{:S(2)}) %collective-permute-start.1) | collective-permute-done | bytes 8224 | tf_op jit(solution)/shard_map/ppermute | solution.py:314
  86.8 0.6 maximum_bitcast_fusion
Async XLA Ops:
  5.7 65.3 %copy-start = (s32[4096]{0:T(1024)S(1)}, s32[4096]{0:T(1024)}, u32[]{:S(2)}) copy-start(s32[4096]{0:T(1024)} %param.5) | copy-start | bytes 49156
  70.1 8.8 %collective-permute-start = (bf16[2048,1024]{1,0:T(8,128)(2,1)}, bf16[2048,1024]{1,0:T(8,128)(2,1)}, u32[]{:S(2)}, u32[]{:S(2)}) collective-permute-start(bf16[2048,1024]{1,0:T(8,128)(2,1)} %bitcast.3.own_hbm), channel_id=1, source_target_pairs={{0,1},{1,0},{2,3},{3,2},{4,5},{5,4},{6,7},{7,6},{8,9},{9,8},{10,11... | collective-permute-start | bytes 12582920 | tf_op jit(solution)/shard_map/ppermute | solution.py:280
  85.6 1.3 %collective-permute-start.1 = (f32[16,128]{1,0:T(8,128)S(1)}, f32[16,128]{1,0:T(8,128)S(1)}, u32[]{:S(2)}, u32[]{:S(2)}) collective-permute-start(f32[16,128]{1,0:T(8,128)S(1)} %get-tuple-element.12), channel_id=1, source_target_pairs={{0,1},{1,0},{2,3},{3,2},{4,5},{5,4},{6,7},{7,6},{8,9},{9,8},{10,11... | collective-permute-start | bytes 24584 | tf_op jit(solution)/shard_map/ppermute | solution.py:314

commit v4 on v3

--- a/solution.py
+++ b/solution.py
@@ -10,7 +10,8 @@
 STRIDE = SUBLANES + 1
 BLOCK = 256
 PARTS = 4
-SPAN = 1024
+OWN_WAITS = {0: 2, 2: 8}
+CROSS_WAITS = {0: 2, 2: 8}
 UNROLL = 128
 ROWS_BY_ROWS = (((1,), (1,)), ((), ()))
 
@@ -145,47 +146,64 @@
     write(rows - UNROLL)
 
 
-def matched(left, right, down, along):
-    scores = lax.dot_general(left, right, ROWS_BY_ROWS, preferred_element_type=jnp.float32)
+def products(left, right):
+    return lax.dot_general(left, right, ROWS_BY_ROWS, preferred_element_type=jnp.float32)
+
+
+def matched(scores, down, along):
     keep = [down == along[:, j : j + LANES] for j in range(0, along.shape[1], LANES)]
     return jnp.where(jnp.concatenate(keep, axis=1), scores, -1.0)
 
 
-def own_column(own_ref, down, along, start):
-    height = start + BLOCK
-    kept = matched(
-        own_ref[pl.ds(0, height), :],
-        own_ref[pl.ds(start, BLOCK), :],
-        down[:height],
-        along[:, start : start + BLOCK],
-    )
-    row_id = lax.broadcasted_iota(jnp.int32, (height, BLOCK), 0)
-    column_id = lax.broadcasted_iota(jnp.int32, (height, BLOCK), 1) + start
-    return jnp.where(row_id != column_id, kept, -1.0)
-
-
-def own_pairs_kernel(side_ref, labels_ref, own_hbm, best_ref, own_ref, fold_ref, sem):
-    rows = own_ref.shape[0]
+def copies_in(source, target, sem):
+    rows = target.shape[0]
     copies = [
         pltpu.make_async_copy(
-            own_hbm.at[pl.ds(start, SPAN), :], own_ref.at[pl.ds(start, SPAN), :], sem.at[i]
+            source.at[pl.ds(start, BLOCK), :], target.at[pl.ds(start, BLOCK), :], sem.at[i]
         )
-        for i, start in enumerate(range(0, rows, SPAN))
+        for i, start in enumerate(range(0, rows, BLOCK))
     ]
     for copy in copies:
         copy.start()
+    return copies
+
+
+def pipelined(score, reduce, copies, waits):
+    scores = None
+    for i in range(len(copies)):
+        if i in waits:
+            for copy in copies[i : waits[i]]:
+                copy.wait()
+        ahead = score(i * BLOCK)
+        if scores is not None:
+            reduce(scores, (i - 1) * BLOCK)
+        scores = ahead
+    reduce(scores, (len(copies) - 1) * BLOCK)
+
+
+def own_pairs_kernel(side_ref, labels_ref, own_hbm, best_ref, own_ref, fold_ref, sem):
+    rows = own_ref.shape[0]
+    copies = copies_in(own_hbm, own_ref, sem)
     labels = labels_ref[:, pl.ds(pl.multiple_of(side_ref[0] * rows, rows), rows)]
     down = down_lanes(labels)
     along = jnp.where(labels < 0, -3, labels)
     fold_ref[...] = jnp.full(fold_ref.shape, -1.0, jnp.float32)
     columns = []
-    for start in range(0, rows, BLOCK):
-        if start % SPAN == 0:
-            copies[start // SPAN].wait()
-        kept = own_column(own_ref, down, along, start)
+
+    def score(start):
+        return products(own_ref[pl.ds(0, start + BLOCK), :], own_ref[pl.ds(start, BLOCK), :])
+
+    def reduce(scores, start):
+        height = start + BLOCK
+        kept = matched(scores, down[:height], along[:, start : start + BLOCK])
+        row_id = lax.broadcasted_iota(jnp.int32, (height, BLOCK), 0)
+        column_id = lax.broadcasted_iota(jnp.int32, (height, BLOCK), 1) + start
+        kept = jnp.where(row_id != column_id, kept, -1.0)
         columns.append(along_lanes(jnp.max(kept, axis=0, keepdims=True)))
-        part = pl.ds(0, start + BLOCK)
+        part = pl.ds(0, height)
         fold_ref[part, :] = jnp.maximum(fold_ref[part, :], fold_lanes(kept))
+
+    pipelined(score, reduce, copies, OWN_WAITS)
     best_ref[...] = jnp.maximum(jnp.concatenate(columns, axis=0), across(fold_ref[...]))
 
 
@@ -196,39 +214,37 @@
     half = rows // 2
     tiles = half // LANES
     side = side_ref[0]
-    copies = [
-        pltpu.make_async_copy(
-            other_hbm.at[pl.ds(start, half), :], other_ref.at[pl.ds(start, half), :], sem.at[i]
-        )
-        for i, start in enumerate(range(0, rows, half))
-    ]
-    for copy in copies:
-        copy.start()
-
+    copies = copies_in(other_hbm, other_ref, sem)
+    firsts, downs, alongs = [], [], []
     for turn in range(2):
-        mine = side ^ turn
-        first = pl.multiple_of(mine * half, half)
+        first = pl.multiple_of((side ^ turn) * half, half)
         own_labels = labels_ref[:, pl.ds(pl.multiple_of(side * rows + first, half), half)]
         other_labels = labels_ref[
             :, pl.ds(pl.multiple_of((1 - side) * rows + turn * half, half), half)
         ]
-        down = down_lanes(own_labels)
-        along = jnp.where(other_labels < 0, -3, other_labels)
-        fold = jnp.full((half, LANES), -1.0, jnp.float32)
-        columns = []
-        copies[turn].wait()
-        for start in range(0, half, BLOCK):
-            kept = matched(
-                own_ref[pl.ds(first, half), :],
-                other_ref[pl.ds(turn * half + start, BLOCK), :],
-                down,
-                along[:, start : start + BLOCK],
-            )
-            columns.append(along_lanes(jnp.max(kept, axis=0, keepdims=True)))
-            fold = jnp.maximum(fold, fold_lanes(kept))
-        other_best_ref[pl.ds(turn * tiles, tiles), :] = jnp.concatenate(columns, axis=0)
-        part = pl.ds(pl.multiple_of(mine * tiles, tiles), tiles)
-        own_best_ref[part, :] = jnp.maximum(best_ref[part, :], across(fold))
+        firsts.append(first)
+        downs.append(down_lanes(own_labels))
+        alongs.append(jnp.where(other_labels < 0, -3, other_labels))
+    columns = []
+    folds = [None, None]
+
+    def score(start):
+        first = firsts[start // half]
+        return products(own_ref[pl.ds(first, half), :], other_ref[pl.ds(start, BLOCK), :])
+
+    def reduce(scores, start):
+        turn = start // half
+        begin = start - turn * half
+        kept = matched(scores, downs[turn], alongs[turn][:, begin : begin + BLOCK])
+        columns.append(along_lanes(jnp.max(kept, axis=0, keepdims=True)))
+        fold = fold_lanes(kept)
+        folds[turn] = fold if folds[turn] is None else jnp.maximum(folds[turn], fold)
+
+    pipelined(score, reduce, copies, CROSS_WAITS)
+    other_best_ref[...] = jnp.concatenate(columns, axis=0)
+    for turn in range(2):
+        part = pl.ds(pl.multiple_of((side ^ turn) * tiles, tiles), tiles)
+        own_best_ref[part, :] = jnp.maximum(best_ref[part, :], across(folds[turn]))
 
 
 def vmem():
@@ -286,7 +302,7 @@
         out_specs=[vmem(), vmem()],
         scratch_shapes=[
             pltpu.VMEM((rows, LANES), jnp.float32),
-            pltpu.SemaphoreType.DMA((rows // SPAN,)),
+            pltpu.SemaphoreType.DMA((rows // BLOCK,)),
         ],
         compiler_params=pltpu.CompilerParams(vmem_limit_bytes=26 << 20),
         cost_estimate=pl.CostEstimate(
@@ -302,7 +318,7 @@
         out_specs=[vmem(), vmem()],
         scratch_shapes=[
             pltpu.VMEM((rows, width), jnp.bfloat16),
-            pltpu.SemaphoreType.DMA((2,)),
+            pltpu.SemaphoreType.DMA((rows // BLOCK,)),
         ],
         compiler_params=pltpu.CompilerParams(vmem_limit_bytes=26 << 20),
         cost_estimate=pl.CostEstimate(

time: 87.6 us -> 86.8 us (level)
  no operation moved by 1% of the time
where the time goes in v4:
time: 86.8 us; the launch traced here: 86.6 us
  blocking collectives  64.4 us (74%)
  Pallas kernels  19.4 us (22%)
  waiting for transfers between devices  1.1 us (1%)
  starting transfers between devices  1.09 us (1%)
    all_to_all x1, blocking collectives, per_device(): lax.all_to_all(unit, ('shard', 'grp'), split_axis=0, concat_axis=0, tiled...  64.4 us
    pallas_call x1, Pallas kernels, per_device(): pl.pallas_call(own_pairs_kernel, out_shape=[best_shape, row_shape], in_sp...  7.39 us
    pallas_call x1, Pallas kernels, per_device(): pl.pallas_call(cross_pairs_kernel, out_shape=[best_shape, best_shape], in...  6.35 us
    pallas_call x1, Pallas kernels, per_device(): pl.pallas_call(unit_rows_kernel, out_shape=pltpu.VMEM((rows, width), jnp....  5.66 us
  transfers between devices with their start and end apart: 2, of which 1 were waited for; matrix products, arithmetic and copies ran while one was open for 0% of the time, Pallas kernels for 9%

profile of v4, /device:TPU:1, one launch (start us, length us, event | category | flops | bytes accessed | tf_op | source)
XLA Modules:
  0.0 86.6 jit_solution(10186433678900486046)
XLA Ops:
  0.0 5.7 %unit_rows.1 = bf16[2048,1024]{1,0:T(8,128)(2,1)S(1)} custom-call(s32[1,2048]{1,0:T(1,128)} %index_ref.1, bf16[2048,1024]{1,0:T(8,128)(2,1)} %rows_ref.1), custom_call_target="tpu_custom_call" | custom-call | flops 16777216 | bytes 8388608 | tf_op jit(solution)/shard_map/unit_rows/pallas_call | solution.py:271
  5.7 0.0 copy-start
  5.7 64.4 %all_to_all.11 = bf16[128,16,1024]{2,1,0:T(8,128)(2,1)} all-to-all(bf16[128,16,1024]{2,1,0:T(8,128)(2,1)S(1)} %bitcast.6), channel_id=1, replica_groups=mesh['shard'=64,'grp'=2] {'shard','grp'}, dimensions={0} | all-to-all | bytes 8388608 | tf_op jit(solution)/shard_map/all_to_all | solution.py:295
  70.1 0.9 %collective-permute-start = (bf16[2048,1024]{1,0:T(8,128)(2,1)}, bf16[2048,1024]{1,0:T(8,128)(2,1)}, u32[]{:S(2)}, u32[]{:S(2)}) collective-permute-start(bf16[2048,1024]{1,0:T(8,128)(2,1)} %bitcast.3.own_hbm), channel_id=1, source_target_pairs={{0,1},{1,0},{2,3},{3,2},{4,5},{5,4},{6,7},{7,6},{8,9},{9,8},{10,11... | collective-permute-start | bytes 12582920 | tf_op jit(solution)/shard_map/ppermute | solution.py:296
  71.0 0.0 copy-done
  71.0 7.4 %own_pairs.1 = (f32[16,128]{1,0:T(8,128)S(1)}, bf16[2048,1024]{1,0:T(8,128)(2,1)S(1)}) custom-call(s32[1]{0:T(128)} %bitcast.side_ref, s32[1,4096]{1,0:T(1,128)S(1)} %bitcast.7, bf16[2048,1024]{1,0:T(8,128)(2,1)} %bitcast.3.own_hbm), custom_call_target="tpu_custom_call" | custom-call | flops 4294967296 | bytes 4194304 | tf_op jit(solution)/shard_map/own_pairs/pallas_call | solution.py:298
  78.4 0.0 collective-permute-done.other_hbm
  78.4 6.4 %cross_pairs.1 = (f32[16,128]{1,0:T(8,128)S(1)}, f32[16,128]{1,0:T(8,128)S(1)}) custom-call(s32[1]{0:T(128)} %bitcast.side_ref, s32[1,4096]{1,0:T(1,128)S(1)} %bitcast.8, f32[16,128]{1,0:T(8,128)S(1)} %get-tuple-element.9.best_ref, bf16[2048,1024]{1,0:T(8,128)(2,1)S(1)} %get-tuple-element.10.own_ref, bf16[2048,1024]{1,0:T(8,128)(2,1)} %collective-permute-done.other_hbm), custom_call_target="tpu_custom_call" | custom-call | flops 4294967296 | bytes 8388608 | tf_op jit(solution)/shard_map/cross_pairs/pallas_call | solution.py:314
  84.8 0.2 collective-permute-start.1
  84.9 1.1 %collective-permute-done.1 = f32[16,128]{1,0:T(8,128)S(1)} collective-permute-done((f32[16,128]{1,0:T(8,128)S(1)}, f32[16,128]{1,0:T(8,128)S(1)}, u32[]{:S(2)}, u32[]{:S(2)}) %collective-permute-start.1) | collective-permute-done | bytes 8224 | tf_op jit(solution)/shard_map/ppermute | solution.py:330
  86.0 0.6 maximum_bitcast_fusion
Async XLA Ops:
  5.7 65.3 %copy-start = (s32[4096]{0:T(1024)S(1)}, s32[4096]{0:T(1024)}, u32[]{:S(2)}) copy-start(s32[4096]{0:T(1024)} %param.5) | copy-start | bytes 49156
  70.1 8.3 %collective-permute-start = (bf16[2048,1024]{1,0:T(8,128)(2,1)}, bf16[2048,1024]{1,0:T(8,128)(2,1)}, u32[]{:S(2)}, u32[]{:S(2)}) collective-permute-start(bf16[2048,1024]{1,0:T(8,128)(2,1)} %bitcast.3.own_hbm), channel_id=1, source_target_pairs={{0,1},{1,0},{2,3},{3,2},{4,5},{5,4},{6,7},{7,6},{8,9},{9,8},{10,11... | collective-permute-start | bytes 12582920 | tf_op jit(solution)/shard_map/ppermute | solution.py:296
  84.8 1.3 %collective-permute-start.1 = (f32[16,128]{1,0:T(8,128)S(1)}, f32[16,128]{1,0:T(8,128)S(1)}, u32[]{:S(2)}, u32[]{:S(2)}) collective-permute-start(f32[16,128]{1,0:T(8,128)S(1)} %get-tuple-element.12), channel_id=1, source_target_pairs={{0,1},{1,0},{2,3},{3,2},{4,5},{5,4},{6,7},{7,6},{8,9},{9,8},{10,11... | collective-permute-start | bytes 24584 | tf_op jit(solution)/shard_map/ppermute | solution.py:330

commit v5 on v4

--- a/solution.py
+++ b/solution.py
@@ -239,12 +239,12 @@
         columns.append(along_lanes(jnp.max(kept, axis=0, keepdims=True)))
         fold = fold_lanes(kept)
         folds[turn] = fold if folds[turn] is None else jnp.maximum(folds[turn], fold)
+        if begin + BLOCK == half:
+            part = pl.ds(pl.multiple_of((side ^ turn) * tiles, tiles), tiles)
+            own_best_ref[part, :] = jnp.maximum(best_ref[part, :], across(folds[turn]))
 
     pipelined(score, reduce, copies, CROSS_WAITS)
     other_best_ref[...] = jnp.concatenate(columns, axis=0)
-    for turn in range(2):
-        part = pl.ds(pl.multiple_of((side ^ turn) * tiles, tiles), tiles)
-        own_best_ref[part, :] = jnp.maximum(best_ref[part, :], across(folds[turn]))
 
 
 def vmem():
@@ -276,7 +276,7 @@
         scratch_shapes=[
             pltpu.VMEM((rows, width), jnp.bfloat16),
             pltpu.VMEM(((groups + 1) * (tiles + 1) * STRIDE, LANES), jnp.float32),
-            pltpu.VMEM((groups * tiles * STRIDE, LANES), jnp.float32),
+            pltpu.VMEM(((groups + 1) * tiles * STRIDE, LANES), jnp.float32),
             pltpu.VMEM((rows, LANES), jnp.float32),
             pltpu.VMEM((1, rows), jnp.int32),
             pltpu.VMEM((1, rows), jnp.int32),

time: 86.8 us -> 86.8 us (level)
  no operation moved by 1% of the time
where the time goes in v5:
time: 86.8 us; the launch traced here: 86.6 us
  blocking collectives  64.4 us (74%)
  Pallas kernels  19.4 us (22%)
  waiting for transfers between devices  1.1 us (1%)
  starting transfers between devices  1.09 us (1%)
    all_to_all x1, blocking collectives, per_device(): lax.all_to_all(unit, ('shard', 'grp'), split_axis=0, concat_axis=0, tiled...  64.4 us
    pallas_call x1, Pallas kernels, per_device(): pl.pallas_call(own_pairs_kernel, out_shape=[best_shape, row_shape], in_sp...  7.39 us
    pallas_call x1, Pallas kernels, per_device(): pl.pallas_call(cross_pairs_kernel, out_shape=[best_shape, best_shape], in...  6.35 us
    pallas_call x1, Pallas kernels, per_device(): pl.pallas_call(unit_rows_kernel, out_shape=pltpu.VMEM((rows, width), jnp....  5.66 us
  transfers between devices with their start and end apart: 2, of which 1 were waited for; matrix products, arithmetic and copies ran while one was open for 0% of the time, Pallas kernels for 9%

profile of v5, /device:TPU:1, one launch (start us, length us, event | category | flops | bytes accessed | tf_op | source)
XLA Modules:
  0.0 86.6 jit_solution(11452580190629538331)
XLA Ops:
  0.0 5.7 %unit_rows.1 = bf16[2048,1024]{1,0:T(8,128)(2,1)S(1)} custom-call(s32[1,2048]{1,0:T(1,128)} %index_ref.1, bf16[2048,1024]{1,0:T(8,128)(2,1)} %rows_ref.1), custom_call_target="tpu_custom_call" | custom-call | flops 16777216 | bytes 8388608 | tf_op jit(solution)/shard_map/unit_rows/pallas_call | solution.py:271
  5.7 0.0 copy-start
  5.7 64.4 %all_to_all.11 = bf16[128,16,1024]{2,1,0:T(8,128)(2,1)} all-to-all(bf16[128,16,1024]{2,1,0:T(8,128)(2,1)S(1)} %bitcast.6), channel_id=1, replica_groups=mesh['shard'=64,'grp'=2] {'shard','grp'}, dimensions={0} | all-to-all | bytes 8388608 | tf_op jit(solution)/shard_map/all_to_all | solution.py:295
  70.1 0.9 %collective-permute-start = (bf16[2048,1024]{1,0:T(8,128)(2,1)}, bf16[2048,1024]{1,0:T(8,128)(2,1)}, u32[]{:S(2)}, u32[]{:S(2)}) collective-permute-start(bf16[2048,1024]{1,0:T(8,128)(2,1)} %bitcast.3.own_hbm), channel_id=1, source_target_pairs={{0,1},{1,0},{2,3},{3,2},{4,5},{5,4},{6,7},{7,6},{8,9},{9,8},{10,11... | collective-permute-start | bytes 12582920 | tf_op jit(solution)/shard_map/ppermute | solution.py:296
  71.0 0.0 copy-done
  71.0 7.4 %own_pairs.1 = (f32[16,128]{1,0:T(8,128)S(1)}, bf16[2048,1024]{1,0:T(8,128)(2,1)S(1)}) custom-call(s32[1]{0:T(128)} %bitcast.side_ref, s32[1,4096]{1,0:T(1,128)S(1)} %bitcast.7, bf16[2048,1024]{1,0:T(8,128)(2,1)} %bitcast.3.own_hbm), custom_call_target="tpu_custom_call" | custom-call | flops 4294967296 | bytes 4194304 | tf_op jit(solution)/shard_map/own_pairs/pallas_call | solution.py:298
  78.4 0.0 collective-permute-done.other_hbm
  78.4 6.4 %cross_pairs.1 = (f32[16,128]{1,0:T(8,128)S(1)}, f32[16,128]{1,0:T(8,128)S(1)}) custom-call(s32[1]{0:T(128)} %bitcast.side_ref, s32[1,4096]{1,0:T(1,128)S(1)} %bitcast.8, f32[16,128]{1,0:T(8,128)S(1)} %get-tuple-element.9.best_ref, bf16[2048,1024]{1,0:T(8,128)(2,1)S(1)} %get-tuple-element.10.own_ref, bf16[2048,1024]{1,0:T(8,128)(2,1)} %collective-permute-done.other_hbm), custom_call_target="tpu_custom_call" | custom-call | flops 4294967296 | bytes 8388608 | tf_op jit(solution)/shard_map/cross_pairs/pallas_call | solution.py:314
  84.8 0.2 collective-permute-start.1
  84.9 1.1 %collective-permute-done.1 = f32[16,128]{1,0:T(8,128)S(1)} collective-permute-done((f32[16,128]{1,0:T(8,128)S(1)}, f32[16,128]{1,0:T(8,128)S(1)}, u32[]{:S(2)}, u32[]{:S(2)}) %collective-permute-start.1) | collective-permute-done | bytes 8224 | tf_op jit(solution)/shard_map/ppermute | solution.py:330
  86.0 0.6 maximum_bitcast_fusion
Async XLA Ops:
  5.7 65.3 %copy-start = (s32[4096]{0:T(1024)S(1)}, s32[4096]{0:T(1024)}, u32[]{:S(2)}) copy-start(s32[4096]{0:T(1024)} %param.5) | copy-start | bytes 49156
  70.1 8.3 %collective-permute-start = (bf16[2048,1024]{1,0:T(8,128)(2,1)}, bf16[2048,1024]{1,0:T(8,128)(2,1)}, u32[]{:S(2)}, u32[]{:S(2)}) collective-permute-start(bf16[2048,1024]{1,0:T(8,128)(2,1)} %bitcast.3.own_hbm), channel_id=1, source_target_pairs={{0,1},{1,0},{2,3},{3,2},{4,5},{5,4},{6,7},{7,6},{8,9},{9,8},{10,11... | collective-permute-start | bytes 12582920 | tf_op jit(solution)/shard_map/ppermute | solution.py:296
  84.8 1.3 %collective-permute-start.1 = (f32[16,128]{1,0:T(8,128)S(1)}, f32[16,128]{1,0:T(8,128)S(1)}, u32[]{:S(2)}, u32[]{:S(2)}) collective-permute-start(f32[16,128]{1,0:T(8,128)S(1)} %get-tuple-element.12), channel_id=1, source_target_pairs={{0,1},{1,0},{2,3},{3,2},{4,5},{5,4},{6,7},{7,6},{8,9},{9,8},{10,11... | collective-permute-start | bytes 24584 | tf_op jit(solution)/shard_map/ppermute | solution.py:330

commit v6 on v5

--- a/solution.py
+++ b/solution.py
@@ -196,9 +196,10 @@
     def reduce(scores, start):
         height = start + BLOCK
         kept = matched(scores, down[:height], along[:, start : start + BLOCK])
-        row_id = lax.broadcasted_iota(jnp.int32, (height, BLOCK), 0)
-        column_id = lax.broadcasted_iota(jnp.int32, (height, BLOCK), 1) + start
-        kept = jnp.where(row_id != column_id, kept, -1.0)
+        row_id = lax.broadcasted_iota(jnp.int32, (BLOCK, BLOCK), 0)
+        column_id = lax.broadcasted_iota(jnp.int32, (BLOCK, BLOCK), 1)
+        square = jnp.where(row_id != column_id, kept[start:], -1.0)
+        kept = jnp.concatenate([kept[:start], square], axis=0) if start else square
         columns.append(along_lanes(jnp.max(kept, axis=0, keepdims=True)))
         part = pl.ds(0, height)
         fold_ref[part, :] = jnp.maximum(fold_ref[part, :], fold_lanes(kept))

time: 86.8 us -> 86.8 us (level)
  no operation moved by 1% of the time
where the time goes in v6:
time: 86.8 us; the launch traced here: 86.6 us
  blocking collectives  64.4 us (74%)
  Pallas kernels  19.4 us (22%)
  waiting for transfers between devices  1.1 us (1%)
  starting transfers between devices  1.09 us (1%)
    all_to_all x1, blocking collectives, per_device(): lax.all_to_all(unit, ('shard', 'grp'), split_axis=0, concat_axis=0, tiled...  64.4 us
    pallas_call x1, Pallas kernels, per_device(): pl.pallas_call(own_pairs_kernel, out_shape=[best_shape, row_shape], in_sp...  7.4 us
    pallas_call x1, Pallas kernels, per_device(): pl.pallas_call(cross_pairs_kernel, out_shape=[best_shape, best_shape], in...  6.35 us
    pallas_call x1, Pallas kernels, per_device(): pl.pallas_call(unit_rows_kernel, out_shape=pltpu.VMEM((rows, width), jnp....  5.66 us
  transfers between devices with their start and end apart: 2, of which 1 were waited for; matrix products, arithmetic and copies ran while one was open for 0% of the time, Pallas kernels for 9%

profile of v6, /device:TPU:1, one launch (start us, length us, event | category | flops | bytes accessed | tf_op | source)
XLA Modules:
  0.0 86.6 jit_solution(1691916618624229671)
XLA Ops:
  0.0 5.7 %unit_rows.1 = bf16[2048,1024]{1,0:T(8,128)(2,1)S(1)} custom-call(s32[1,2048]{1,0:T(1,128)} %index_ref.1, bf16[2048,1024]{1,0:T(8,128)(2,1)} %rows_ref.1), custom_call_target="tpu_custom_call" | custom-call | flops 16777216 | bytes 8388608 | tf_op jit(solution)/shard_map/unit_rows/pallas_call | solution.py:272
  5.7 0.0 copy-start
  5.7 64.4 %all_to_all.11 = bf16[128,16,1024]{2,1,0:T(8,128)(2,1)} all-to-all(bf16[128,16,1024]{2,1,0:T(8,128)(2,1)S(1)} %bitcast.6), channel_id=1, replica_groups=mesh['shard'=64,'grp'=2] {'shard','grp'}, dimensions={0} | all-to-all | bytes 8388608 | tf_op jit(solution)/shard_map/all_to_all | solution.py:296
  70.1 0.9 %collective-permute-start = (bf16[2048,1024]{1,0:T(8,128)(2,1)}, bf16[2048,1024]{1,0:T(8,128)(2,1)}, u32[]{:S(2)}, u32[]{:S(2)}) collective-permute-start(bf16[2048,1024]{1,0:T(8,128)(2,1)} %bitcast.3.own_hbm), channel_id=1, source_target_pairs={{0,1},{1,0},{2,3},{3,2},{4,5},{5,4},{6,7},{7,6},{8,9},{9,8},{10,11... | collective-permute-start | bytes 12582920 | tf_op jit(solution)/shard_map/ppermute | solution.py:297
  71.0 0.0 copy-done
  71.0 7.4 %own_pairs.1 = (f32[16,128]{1,0:T(8,128)S(1)}, bf16[2048,1024]{1,0:T(8,128)(2,1)S(1)}) custom-call(s32[1]{0:T(128)} %bitcast.side_ref, s32[1,4096]{1,0:T(1,128)S(1)} %bitcast.7, bf16[2048,1024]{1,0:T(8,128)(2,1)} %bitcast.3.own_hbm), custom_call_target="tpu_custom_call" | custom-call | flops 4294967296 | bytes 4194304 | tf_op jit(solution)/shard_map/own_pairs/pallas_call | solution.py:299
  78.4 0.0 collective-permute-done.other_hbm
  78.4 6.3 %cross_pairs.1 = (f32[16,128]{1,0:T(8,128)S(1)}, f32[16,128]{1,0:T(8,128)S(1)}) custom-call(s32[1]{0:T(128)} %bitcast.side_ref, s32[1,4096]{1,0:T(1,128)S(1)} %bitcast.8, f32[16,128]{1,0:T(8,128)S(1)} %get-tuple-element.9.best_ref, bf16[2048,1024]{1,0:T(8,128)(2,1)S(1)} %get-tuple-element.10.own_ref, bf16[2048,1024]{1,0:T(8,128)(2,1)} %collective-permute-done.other_hbm), custom_call_target="tpu_custom_call" | custom-call | flops 4294967296 | bytes 8388608 | tf_op jit(solution)/shard_map/cross_pairs/pallas_call | solution.py:315
  84.8 0.2 collective-permute-start.1
  84.9 1.1 %collective-permute-done.1 = f32[16,128]{1,0:T(8,128)S(1)} collective-permute-done((f32[16,128]{1,0:T(8,128)S(1)}, f32[16,128]{1,0:T(8,128)S(1)}, u32[]{:S(2)}, u32[]{:S(2)}) %collective-permute-start.1) | collective-permute-done | bytes 8224 | tf_op jit(solution)/shard_map/ppermute | solution.py:331
  86.0 0.6 maximum_bitcast_fusion
Async XLA Ops:
  5.7 65.3 %copy-start = (s32[4096]{0:T(1024)S(1)}, s32[4096]{0:T(1024)}, u32[]{:S(2)}) copy-start(s32[4096]{0:T(1024)} %param.5) | copy-start | bytes 49156
  70.1 8.3 %collective-permute-start = (bf16[2048,1024]{1,0:T(8,128)(2,1)}, bf16[2048,1024]{1,0:T(8,128)(2,1)}, u32[]{:S(2)}, u32[]{:S(2)}) collective-permute-start(bf16[2048,1024]{1,0:T(8,128)(2,1)} %bitcast.3.own_hbm), channel_id=1, source_target_pairs={{0,1},{1,0},{2,3},{3,2},{4,5},{5,4},{6,7},{7,6},{8,9},{9,8},{10,11... | collective-permute-start | bytes 12582920 | tf_op jit(solution)/shard_map/ppermute | solution.py:297
  84.8 1.3 %collective-permute-start.1 = (f32[16,128]{1,0:T(8,128)S(1)}, f32[16,128]{1,0:T(8,128)S(1)}, u32[]{:S(2)}, u32[]{:S(2)}) collective-permute-start(f32[16,128]{1,0:T(8,128)S(1)} %get-tuple-element.12), channel_id=1, source_target_pairs={{0,1},{1,0},{2,3},{3,2},{4,5},{5,4},{6,7},{7,6},{8,9},{9,8},{10,11... | collective-permute-start | bytes 24584 | tf_op jit(solution)/shard_map/ppermute | solution.py:331
